TPU v7x, 256 devices: a whole 4x4x8 slice. The times are simulated.
256 devices in a mesh: ctx: 32 (over z, x), head: 8 (over y, core).
Axes of the slice: x: 4, y: 4, z: 8, core: 2. Of those that a mesh axis runs over, the one named last changes fastest.
Arguments:
- queries: bfloat16 [98304, 1024], P('ctx', 'head'), may hold values from -6 to 6
- keys: bfloat16 [98304, 1024], P('ctx', 'head'), may hold values from -6 to 6
- values: bfloat16 [98304, 1024], P('ctx', 'head'), may hold values from -6 to 6
- prefix: int32 [1], replicated, may hold values from 24576 to 73727
- norm_gain: float32 [1024], P('head'), may hold values from 0.1 to 1.9
- out_weight: bfloat16 [1024, 4096], P(None, 'head'), may hold values from -0.1875 to 0.1875
Outputs:
- projected: bfloat16 [98304, 4096], P('ctx', 'head')
All inputs are finite; a program needn't handle non-finite values.
Results may differ from a plain program's by a relative error of at most 0.0049.
Values may be sent and summed in bfloat16 or wider, within the bound.
A program may use at most 64 MiB of HBM per device.

v0:
```python
import jax
import jax.numpy as jnp
from jax import lax
from jax.sharding import PartitionSpec as P

HD = 128
GROUP = 512


def prefix_2(part, axis, combine, identity):
    place = lax.axis_index(axis)
    gathered = lax.all_gather(part, axis)
    state = jnp.zeros_like(part) + jnp.asarray(identity, part.dtype)

    def one(hop, state):
        return combine(state, lax.dynamic_index_in_dim(gathered, hop, 0, False))

    return lax.fori_loop(0, place, one, state)


def add_states(preceding_tokens, later):
    return preceding_tokens + later


def body(queries, keys, values, prefix, norm_gain, out_weight):
    row_count, feature_dimension = queries.shape
    local_heads = feature_dimension // HD
    blocks = row_count // GROUP
    leading_token = lax.axis_index("ctx") * row_count
    positions = leading_token + jnp.arange(row_count, dtype=jnp.int32)
    inside = (positions < prefix[0]).reshape(blocks, GROUP)
    query_blocks = queries.reshape(blocks, GROUP, local_heads, HD)
    key_blocks = keys.reshape(blocks, GROUP, local_heads, HD)
    value_blocks = values.reshape(blocks, GROUP, local_heads, HD)
    block_states = jnp.einsum(
        "nchd,nche->nhde", key_blocks, value_blocks, preferred_element_type=jnp.float32
    )
    masked_keys = key_blocks * inside[:, :, None, None].astype(jnp.bfloat16)
    masked_state = jnp.sum(
        jnp.einsum(
            "nchd,nche->nhde", masked_keys, value_blocks, preferred_element_type=jnp.float32
        ),
        axis=0,
    )
    local_state = jnp.sum(block_states, axis=0)
    carried = prefix_2(local_state, "ctx", add_states, jnp.zeros_like(local_state))
    prefix_state = lax.psum(masked_state, "ctx")
    running = jnp.cumsum(block_states, axis=0)
    prior = carried[None] + jnp.concatenate(
        [jnp.zeros_like(block_states[:1]), running[:-1]], axis=0
    )
    whole_inside = inside[:, -1]
    chosen_state = jnp.where(whole_inside[:, None, None, None], prefix_state[None], prior)
    query_as_float = query_blocks.astype(jnp.float32)
    preceding_tokens = jnp.einsum(
        "nchd,nhde->nche", query_as_float, chosen_state, precision=lax.Precision.HIGHEST
    )
    straddle = jnp.clip((prefix[0] - leading_token) // GROUP, 0, blocks - 1)
    straddle_query = lax.dynamic_slice_in_dim(query_as_float, straddle, 1, 0)
    straddle_read = jnp.einsum(
        "nchd,hde->nche", straddle_query, prefix_state, precision=lax.Precision.HIGHEST
    )
    prefix_fill = lax.dynamic_update_slice_in_dim(preceding_tokens, straddle_read, straddle, 0)
    attention_scores = jnp.einsum(
        "nchd,nmhd->nhcm", query_blocks, key_blocks, preferred_element_type=jnp.float32
    )
    lower_mask = jnp.tril(jnp.ones((GROUP, GROUP), dtype=bool))
    weights = jnp.where(lower_mask[None, None], attention_scores, 0.0).astype(jnp.bfloat16)
    local_part = jnp.einsum(
        "nhcm,nmhe->nche", weights, value_blocks, preferred_element_type=jnp.float32
    )
    attended = jnp.where(inside[:, :, None, None], prefix_fill, preceding_tokens + local_part)
    mean_square = jnp.mean(attended * attended, axis=-1, keepdims=True)
    head_normalized = attended * lax.rsqrt(mean_square + 1e-06) * norm_gain.reshape(local_heads, HD)
    head_normalized = head_normalized.astype(jnp.bfloat16).reshape(row_count, feature_dimension)
    projected = jnp.dot(
        lax.all_gather(head_normalized, "head", axis=1, tiled=True),
        out_weight,
        preferred_element_type=jnp.float32,
    )
    return projected.astype(jnp.bfloat16)


def solution(mesh):
    return jax.shard_map(
        body,
        mesh=mesh,
        in_specs=(
            P("ctx", "head"),
            P("ctx", "head"),
            P("ctx", "head"),
            P(),
            P("head"),
            P(None, "head"),
        ),
        out_specs=P("ctx", "head"),
        check_vma=False,
    )
```

profile of v0, /device:TPU:1, one launch (start us, length us, event | category | flops | bytes accessed | tf_op | source)
XLA Modules:
  0.0 305.3 jit_solution(16947940067111918171)
XLA Ops:
  6.5 0.0 copy-start
  6.5 0.0 all-gather.6.cloned.1.call-start
  6.5 2.6 fusion.24
  9.1 0.0 all-gather.6.cloned.1.call-update
  9.1 0.0 all-reduce.3.cloned.1.call-start
  9.9 0.0 copy-done.2
  9.9 1.5 convolution_bitcast_fusion.2
  11.4 0.0 all-reduce.3.cloned.1.call-update
  11.4 0.0 all-gather.4.cloned.1.call-start
  11.5 0.1 iota_compare_fusion
  11.6 0.2 slice_reduce_fusion
  11.8 0.3 fusion.9
  12.1 75.6 %all-gather.6.cloned.1.call-done = f32[4096,128]{1,0:T(8,128)} async-done(((f32[128,128]{1,0:T(8,128)}), f32[4096,128]{1,0:T(8,128)}) %all-gather.6.cloned.1.call-update) | async-done | bytes 2097168 | tf_op jit(solution)/shard_map/all_gather | solution.py:12
  87.8 139.6 %all-reduce.3.cloned.1.call-done = f32[128,128]{1,0:T(8,128)} async-done(((f32[128,128]{1,0:T(8,128)}), f32[128,128]{1,0:T(8,128)}) %all-reduce.3.cloned.1.call-update) | async-done | bytes 65552 | tf_op jit(solution)/shard_map/psum | solution.py:47
  227.4 2.1 convolution_bitcast_fusion
  229.5 1.1 copy.41
  230.6 0.0 copy-done.3
  230.6 1.9 fusion.6
  232.6 5.3 %multiply_reduce_fusion = (f32[6,512]{1,0:T(8,128)S(1)}, f32[6,512,1,128]{1,3,0,2:T(8,128)}) fusion(f32[6,512,1,128]{1,3,0,2:T(8,128)} %fusion.6, f32[6,512,1,128]{1,3,0,2:T(8,128)S(1)} %convolution_bitcast_fusion, bf16[6,512,128]{2,1,0:T(8,128)(2,1)} %bitcast.63, pred[512,512]{1,0:T(8,128)(4,1)S(1)} %iota_compare_fusion, ...), kind=kOutput, calls=%fused_computation.10 | convolution fusion | flops 810021888 | bytes 7355392 | tf_op jit(solution)/shard_map/nhcm,nmhe->nche/dot_general | solution.py:69
  237.9 1.8 multiply_convert_fusion
  239.6 1.2 copy.29
  240.8 0.0 all-gather.4.cloned.1.call-update
  240.8 50.4 %all-gather.4.cloned.1.call-done = bf16[3072,1024]{1,0:T(8,128)(2,1)} async-done(((bf16[3072,128]{1,0:T(8,128)(2,1)}), bf16[3072,1024]{1,0:T(8,128)(2,1)}) %all-gather.4.cloned.1.call-update) | async-done | bytes 6291472 | tf_op jit(solution)/shard_map/all_gather | solution.py:77
  291.2 7.5 %convolution_convert_fusion = bf16[3072,512]{1,0:T(8,128)(2,1)} fusion(bf16[3072,1024]{1,0:T(8,128)(2,1)} %all-gather.4.cloned.1.call-done, bf16[1024,512]{1,0:T(8,128)(2,1)S(1)} %copy-done), kind=kOutput, calls=%fused_computation.2 | convolution fusion | flops 3222798336 | bytes 10485760 | tf_op jit(solution)/shard_map/dot_general | solution.py:76
  (13 shorter events, 0.1 us)
Async XLA Ops:
  6.5 284.7 %copy-start = (bf16[1024,512]{1,0:T(8,128)(2,1)S(1)}, bf16[1024,512]{1,0:T(8,128)(2,1)}, u32[]{:S(2)}) copy-start(bf16[1024,512]{1,0:T(8,128)(2,1)} %param.13) | copy-start | bytes 3145732
  6.5 3.3 %copy-start.2 = (bf16[3072,128]{1,0:T(8,128)(2,1)S(1)}, bf16[3072,128]{1,0:T(8,128)(2,1)}, u32[]{:S(2)}) copy-start(bf16[3072,128]{1,0:T(8,128)(2,1)} %param.10) | copy-start | bytes 2359300
  6.5 3.3 %copy-start.1 = (bf16[3072,128]{1,0:T(8,128)(2,1)S(1)}, bf16[3072,128]{1,0:T(8,128)(2,1)}, u32[]{:S(2)}) copy-start(bf16[3072,128]{1,0:T(8,128)(2,1)} %param.9) | copy-start | bytes 2359300
  6.5 81.2 %all-gather.6.cloned.1.call-start = ((), (), s32[]{:S(2)}) async-start(), calls=%async_computation.2 | async-start | bytes 2162688 | tf_op jit(solution)/shard_map/all_gather | solution.py:12
  9.1 218.3 %all-reduce.3.cloned.1.call-start = ((), (), s32[]{:S(2)}) async-start(), calls=%async_computation | async-start | bytes 131072 | tf_op jit(solution)/shard_map/psum | solution.py:47
  11.4 279.8 %all-gather.4.cloned.1.call-start = ((), (), s32[]{:S(2)}) async-start(), calls=%async_computation.1 | async-start | bytes 7077888 | tf_op jit(solution)/shard_map/all_gather | solution.py:77
  229.5 1.2 copy-start.3
  232.6 5.3 %copy-start.4 = (f32[128]{0:T(128)S(1)}, f32[128]{0:T(128)}, u32[]{:S(2)}) copy-start(f32[128]{0:T(128)} %param.12) | copy-start | bytes 1540
Sparse Core Ops, SparseCore 0:
  9.9 77.7 all-gather.5
  91.2 136.1 all-reduce.2
  240.9 50.2 all-gather.3
where the time goes:
time: 307 us; the launch traced here: 305 us
  waiting for transfers between devices  266 us (87%)
  matrix products  20.9 us (7%)
  between operations  13.9 us (5%)
    psum x1, waiting for transfers between devices, body(): prefix_state = lax.psum(masked_state, 'ctx')  140 us
    all_gather x1, waiting for transfers between devices, prefix_2(): gathered = lax.all_gather(part, axis)  75.6 us
    all_gather x1, waiting for transfers between devices, body(): lax.all_gather(head_normalized, 'head', axis=1, tiled=True)  50.4 us
    dot_general x1, matrix products, body(): jnp.dot(lax.all_gather(head_normalized, 'head', axis=1, tiled=True), out_...  7.54 us
  transfers between devices with their start and end apart: 3, of which 3 were waited for; matrix products, arithmetic and copies ran while one was open for 1% of the time, Pallas kernels for 0%

commit v1 on v0

v1 whole, which is shorter than its diff:
```python
import jax
import jax.numpy as jnp
from jax import lax
from jax.experimental import pallas as pl
from jax.experimental.pallas import tpu as pltpu
from jax.sharding import PartitionSpec as P

MESH = pl.DeviceIdType.MESH
HD = 128
X, Y, Z, CORES = 4, 4, 8, 2
HEADS = Y * CORES
ROWS = 3072
COLS = 512
SUB = 256
SUBS = ROWS // SUB
PART = 512
PARTS = ROWS // PART
HALF = PART // 2
AHEAD = 2
QUARTER = HD // X
NT = (((1,), (1,)), ((), ()))
TN = (((0,), (0,)), ((), ()))
F32, BF16 = jnp.float32, jnp.bfloat16

FROM_LEFT, FROM_RIGHT, FAR_A, FAR_B, SIB_OWN, SIB_LEFT, SIB_RIGHT, SIB_A, SIB_B = range(9)


def split_two(x):
    high = x.astype(BF16)
    return jnp.concatenate([high, (x - high.astype(F32)).astype(BF16)], axis=1)


def dot_two(rows, halves):
    both = jnp.dot(rows, halves, preferred_element_type=F32)
    return both[:, :HD] + both[:, HD:]


def kernel(
    q_hbm, k_hbm, v_hbm, prefix_ref, gain_ref, w_hbm, out_hbm,
    q, k, v, w, out, local, gathered, total, earlier, own_masked, read_state,
    got1, sums, got2, give3, got3,
    load_sem, out_sem, ex_send, ex_recv, ring_send, ring_recv,
):
    ctx, head = lax.axis_index("ctx"), lax.axis_index("head")
    z, x = ctx // X, ctx % X
    y, core = head // CORES, head % CORES

    x_peers = [(z * X + (x + s) % X, head) for s in range(1, X)]
    z_peers = [(((z + s) % Z) * X + x, head) for s in range(1, Z)]
    right = (ctx, ((y + 1) % Y) * CORES + core)
    left = (ctx, ((y + Y - 1) % Y) * CORES + core)
    sibling = (ctx, y * CORES + 1 - core)

    barrier = pltpu.get_barrier_semaphore()
    everyone = x_peers + z_peers + [right, left, sibling]
    for peer in everyone:
        pl.semaphore_signal(barrier, inc=1, device_id=peer, device_id_type=MESH)

    loads = [
        pltpu.make_async_copy(src, dst, load_sem.at[i])
        for i, (src, dst) in enumerate([(k_hbm, k), (v_hbm, v), (q_hbm, q), (w_hbm, w)])
    ]
    for load in loads:
        load.start()

    prefix = prefix_ref[0]
    base = ctx * ROWS

    def inside(block):
        at = base + block * SUB + lax.broadcasted_iota(jnp.int32, (SUB, HD), 0)
        return at < prefix

    loads[0].wait()
    loads[1].wait()

    def state(block, carry):
        rows = pl.ds(block * SUB, SUB)
        vals = v[rows, :]
        masked = jnp.where(inside(block), vals, jnp.zeros_like(vals))
        earlier[block] = split_two(carry[:, :HD])
        return carry + lax.dot_general(
            k[rows, :], jnp.concatenate([vals, masked], axis=1), TN, preferred_element_type=F32
        )

    summed = lax.fori_loop(0, SUBS, state, jnp.zeros((HD, 2 * HD), F32))
    total[...] = summed
    own_masked[...] = split_two(summed[:, HD:])
    mine = pl.ds(pl.multiple_of(x * QUARTER, QUARTER), QUARTER)
    got1[x] = total[mine, :]

    pl.semaphore_wait(barrier, len(everyone))

    def exchange(src, dst, slot, peer):
        return pltpu.make_async_remote_copy(
            src_ref=src, dst_ref=dst, send_sem=ex_send.at[slot], recv_sem=ex_recv.at[slot],
            device_id=peer, device_id_type=MESH,
        )

    first = []
    for s in range(1, X):
        quarter = pl.ds(pl.multiple_of(((x + s) % X) * QUARTER, QUARTER), QUARTER)
        first.append(exchange(total.at[quarter], got1.at[x], s - 1, x_peers[s - 1]))
        first[-1].start()

    loads[2].wait()
    row_at = lax.broadcasted_iota(jnp.int32, (SUB, SUB), 0)
    col_at = lax.broadcasted_iota(jnp.int32, (SUB, SUB), 1)

    def causal(block, _):
        rows = pl.ds(block * SUB, SUB)
        queries = q[rows, :]
        scores = lax.dot_general(queries, k[rows, :], NT, preferred_element_type=F32)
        weights = jnp.where(col_at <= row_at, scores, 0.0).astype(BF16)
        near = jnp.dot(weights, v[rows, :], preferred_element_type=F32)
        near = near + dot_two(queries, earlier[block])
        local[rows, :] = jnp.where(inside(block), dot_two(queries, own_masked[...]), near)
        return 0

    lax.fori_loop(0, 4, causal, 0)

    for moved in first:
        moved.wait_recv()
    along_x = got1[0] + got1[1] + got1[2] + got1[3]
    sums[0] = along_x[:, :HD]
    sums[1] = along_x[:, HD:]

    second = []
    for s in range(1, Z):
        second.append(exchange(sums.at[(z + s) // Z], got2.at[s - 1], X - 2 + s, z_peers[s - 1]))
        second[-1].start()

    lax.fori_loop(4, 9, causal, 0)

    for moved in second:
        moved.wait_recv()
    along_z = got2[0]
    for s in range(1, Z - 1):
        along_z = along_z + got2[s]
    for to in range(X):
        part = along_z
        for s in range(X):
            if s < to:
                part = part + got1[s][:, :HD]
            elif s > to:
                part = part + got1[s][:, HD:]
        give3[to] = part
    got3[x] = give3[x]

    third = []
    for s in range(1, X):
        third.append(exchange(give3.at[(x + s) % X], got3.at[x], X + Z - 3 + s, x_peers[s - 1]))
        third[-1].start()

    lax.fori_loop(9, SUBS, causal, 0)

    for moved in third:
        moved.wait_recv()
    read_state[...] = split_two(got3[...].reshape(HD, HD))
    loads[3].wait()

    left_head = ((y + Y - 1) % Y) * CORES + core
    right_head = ((y + 1) % Y) * CORES + core
    far_head = ((y + 2) % Y) * CORES + core

    def copy(block, slot):
        heads, first_row, count, peer = (
            (head, 0, PART, right),
            (head, 0, PART, left),
            (left_head, 0, HALF, right),
            (right_head, HALF, HALF, left),
            (head, 0, PART, sibling),
            (left_head, 0, PART, sibling),
            (right_head, 0, PART, sibling),
            (far_head, 0, HALF, sibling),
            (far_head, HALF, HALF, sibling),
        )[slot]
        piece = gathered.at[heads, pl.ds(pl.multiple_of(block * PART + first_row, HALF), count)]
        return pltpu.make_async_remote_copy(
            src_ref=piece, dst_ref=piece,
            send_sem=ring_send.at[block, slot], recv_sem=ring_recv.at[block, slot],
            device_id=peer, device_id_type=MESH,
        )

    gain = gain_ref[...]

    def norm(block):
        rows = pl.ds(pl.multiple_of(block * PART, PART), PART)
        attended = dot_two(q[rows, :], read_state[...]) + local[rows, :]
        mean_square = jnp.mean(attended * attended, axis=-1, keepdims=True)
        normed = attended * lax.rsqrt(mean_square + 1e-06) * gain
        gathered[head, rows, :] = normed.astype(BF16)
        for slot in (FROM_LEFT, FROM_RIGHT, SIB_OWN):
            copy(block, slot).start()

    def forward(block):
        copy(block, FROM_LEFT).wait_recv()
        copy(block, FAR_A).start()
        copy(block, SIB_LEFT).start()
        copy(block, FROM_RIGHT).wait_recv()
        copy(block, FAR_B).start()
        copy(block, SIB_RIGHT).start()

    def pass_far(block):
        copy(block, FAR_A).wait_recv()
        copy(block, SIB_A).start()
        copy(block, FAR_B).wait_recv()
        copy(block, SIB_B).start()

    def store(block):
        rows = pl.ds(pl.multiple_of(block * PART, PART), PART)
        return pltpu.make_async_copy(out.at[rows], out_hbm.at[rows], out_sem.at[block])

    def project(block):
        for slot in (SIB_OWN, SIB_LEFT, SIB_RIGHT, SIB_A, SIB_B):
            copy(block, slot).wait_recv()
        rows = pl.ds(pl.multiple_of(block * PART, PART), PART)
        normed = jnp.concatenate([gathered[h, rows, :] for h in range(HEADS)], axis=1)
        out[rows, :] = jnp.dot(normed, w[...], preferred_element_type=F32).astype(BF16)
        store(block).start()

    def step(t, _):
        @pl.when(t < PARTS)
        def _():
            norm(t)

        @pl.when((t >= AHEAD) & (t < PARTS + AHEAD))
        def _():
            forward(t - AHEAD)

        @pl.when((t >= AHEAD + 2) & (t < PARTS + AHEAD + 2))
        def _():
            project(t - AHEAD - 2)

        @pl.when((t >= AHEAD + 1) & (t < PARTS + AHEAD + 1))
        def _():
            pass_far(t - AHEAD - 1)

        return 0

    lax.fori_loop(0, PARTS + AHEAD + 2, step, 0)

    for moved in first + second + third:
        moved.wait_send()

    def drain(block, _):
        for slot in range(9):
            copy(block, slot).wait_send()
        store(block).wait()
        return 0

    lax.fori_loop(0, PARTS, drain, 0)


def body(queries, keys, values, prefix, norm_gain, out_weight):
    hbm = pl.BlockSpec(memory_space=pl.ANY)
    exchanges = 2 * (X - 1) + Z - 1
    return pl.pallas_call(
        kernel,
        out_shape=jax.ShapeDtypeStruct((ROWS, COLS), BF16),
        in_specs=[
            hbm, hbm, hbm,
            pl.BlockSpec(memory_space=pltpu.SMEM),
            pl.BlockSpec(memory_space=pltpu.VMEM),
            hbm,
        ],
        out_specs=hbm,
        scratch_shapes=[
            pltpu.VMEM((ROWS, HD), BF16),
            pltpu.VMEM((ROWS, HD), BF16),
            pltpu.VMEM((ROWS, HD), BF16),
            pltpu.VMEM((HEADS * HD, COLS), BF16),
            pltpu.VMEM((ROWS, COLS), BF16),
            pltpu.VMEM((ROWS, HD), F32),
            pltpu.VMEM((HEADS, ROWS, HD), BF16),
            pltpu.VMEM((HD, 2 * HD), F32),
            pltpu.VMEM((SUBS, HD, 2 * HD), BF16),
            pltpu.VMEM((HD, 2 * HD), BF16),
            pltpu.VMEM((HD, 2 * HD), BF16),
            pltpu.VMEM((X, QUARTER, 2 * HD), F32),
            pltpu.VMEM((2, QUARTER, HD), F32),
            pltpu.VMEM((Z - 1, QUARTER, HD), F32),
            pltpu.VMEM((X, QUARTER, HD), F32),
            pltpu.VMEM((X, QUARTER, HD), F32),
            pltpu.SemaphoreType.DMA((4,)),
            pltpu.SemaphoreType.DMA((PARTS,)),
            pltpu.SemaphoreType.DMA((exchanges,)),
            pltpu.SemaphoreType.DMA((exchanges,)),
            pltpu.SemaphoreType.DMA((PARTS, 9)),
            pltpu.SemaphoreType.DMA((PARTS, 9)),
        ],
        compiler_params=pltpu.CompilerParams(
            collective_id=0, has_side_effects=True, vmem_limit_bytes=40 * 2**20
        ),
        cost_estimate=pl.CostEstimate(
            flops=2 * ROWS * (8 * HD * COLS + 1024 * HD), bytes_accessed=8 * 2**20, transcendentals=ROWS
        ),
    )(queries, keys, values, prefix, norm_gain.reshape(1, HD), out_weight)


def solution(mesh):
    return jax.shard_map(
        body,
        mesh=mesh,
        in_specs=(
            P("ctx", "head"),
            P("ctx", "head"),
            P("ctx", "head"),
            P(),
            P("head"),
            P(None, "head"),
        ),
        out_specs=P("ctx", "head"),
        check_vma=False,
    )
```

time: 307 us -> 62.5 us (0.20)
  waiting for transfers between devices: 266 us -> 0 us
  Pallas kernels: 0 us -> 54.6 us
  matrix products: 20.9 us -> 0 us
  between operations: 13.9 us -> 0.67 us
  local copies, waits for them, and re-layouts: 2.53 us -> 6.94 us
    psum x1 -> x0, waiting for transfers between devices: 140 us -> none  [body(): prefix_state = lax.psum(masked_state, 'ctx')]
    all_gather x2 -> x0, waiting for transfers between devices: 126 us -> none  [the longest x1 75.6 us: prefix_2(): gathered = lax.all_gather(part, axis)]
    pallas_call x0 -> x1, Pallas kernels: none -> 54.6 us  [body(): pl.pallas_call(kernel, out_shape=jax.ShapeDtypeStruct((ROWS, COLS), BF16)...]
    dot_general x6 -> x0, matrix products: 20.9 us -> none  [the longest x1 7.54 us: body(): jnp.dot(lax.all_gather(head_normalized, 'head', axis=1, tiled=True), out_...]
    unnamed x11, local copies, waits for them, and re-layouts: 1.16 us -> 6.94 us
  transfers between devices with their start and end apart: 3 -> 0, of which waited for: 3 -> 0; matrix products, arithmetic and copies ran while one was open for 1% -> 0% of each run, Pallas kernels for 0% -> 0%
where the time goes in v1:
time: 62.5 us; the launch traced here: 62.2 us
  Pallas kernels  54.6 us (87%)
  local copies, waits for them, and re-layouts  6.94 us (11%)
  between operations  0.67 us (1%)
    pallas_call x1, Pallas kernels, body(): pl.pallas_call(kernel, out_shape=jax.ShapeDtypeStruct((ROWS, COLS), BF16)...  54.6 us
    unnamed x11, local copies, waits for them, and re-layouts  6.94 us

profile of v1, /device:TPU:1, one launch (start us, length us, event | category | flops | bytes accessed | tf_op | source)
XLA Modules:
  0.0 62.2 jit_solution(15803968354751808035)
XLA Ops:
  0.7 0.0 copy-start
  0.7 1.2 %copy-done = bf16[1024,512]{1,0:T(8,128)(2,1)S(1)} copy-done((bf16[1024,512]{1,0:T(8,128)(2,1)S(1)}, bf16[1024,512]{1,0:T(8,128)(2,1)}, u32[]{:S(2)}) %copy-start) | copy-done | bytes 1048600
  1.9 0.0 copy-start.1
  1.9 1.1 %copy-done.1 = bf16[3072,128]{1,0:T(8,128)(2,1)S(1)} copy-done((bf16[3072,128]{1,0:T(8,128)(2,1)S(1)}, bf16[3072,128]{1,0:T(8,128)(2,1)}, u32[]{:S(2)}) %copy-start.1) | copy-done | bytes 786456
  3.0 0.0 copy-start.2
  3.0 1.1 %copy-done.2 = bf16[3072,128]{1,0:T(8,128)(2,1)S(1)} copy-done((bf16[3072,128]{1,0:T(8,128)(2,1)S(1)}, bf16[3072,128]{1,0:T(8,128)(2,1)}, u32[]{:S(2)}) %copy-start.2) | copy-done | bytes 786456
  4.1 0.0 copy-start.3
  4.1 1.1 %copy-done.3 = bf16[3072,128]{1,0:T(8,128)(2,1)S(1)} copy-done((bf16[3072,128]{1,0:T(8,128)(2,1)S(1)}, bf16[3072,128]{1,0:T(8,128)(2,1)}, u32[]{:S(2)}) %copy-start.3) | copy-done | bytes 786456
  5.3 0.0 copy-start.4
  5.3 0.7 %copy-done.4 = f32[128]{0:T(128)S(1)} copy-done((f32[128]{0:T(128)S(1)}, f32[128]{0:T(128)}, u32[]{:S(2)}) %copy-start.4) | copy-done | bytes 536
  5.9 54.6 %shard_map.64 = bf16[3072,512]{1,0:T(8,128)(2,1)S(1)} custom-call(bf16[3072,128]{1,0:T(8,128)(2,1)S(1)} %copy-done.1, bf16[3072,128]{1,0:T(8,128)(2,1)S(1)} %copy-done.2, bf16[3072,128]{1,0:T(8,128)(2,1)S(1)} %copy-done.3, s32[1]{0:T(128)S(6)} %copy.8.prefix_ref, f32[1,128]{1,0:T(1,128)S(1)} %bitcast.1, bf16[1024,512]{1,0:T(8,128)(2,1)S(1)} %copy-done), custom_call_target="tpu_custom_call" | custom-call | flops 4026531840 | bytes 8388608 | tf_op jit(solution)/shard_map/pallas_call | solution.py:257
  60.5 1.7 %copy.9 = bf16[3072,512]{1,0:T(8,128)(2,1)} copy(bf16[3072,512]{1,0:T(8,128)(2,1)S(1)} %shard_map.64) | data formatting | bytes 6291456
Async XLA Ops:
  0.7 1.2 %copy-start = (bf16[1024,512]{1,0:T(8,128)(2,1)S(1)}, bf16[1024,512]{1,0:T(8,128)(2,1)}, u32[]{:S(2)}) copy-start(bf16[1024,512]{1,0:T(8,128)(2,1)} %w_hbm.1) | copy-start | bytes 3145732
  1.9 1.1 %copy-start.1 = (bf16[3072,128]{1,0:T(8,128)(2,1)S(1)}, bf16[3072,128]{1,0:T(8,128)(2,1)}, u32[]{:S(2)}) copy-start(bf16[3072,128]{1,0:T(8,128)(2,1)} %q_hbm.1) | copy-start | bytes 2359300
  3.0 1.1 %copy-start.2 = (bf16[3072,128]{1,0:T(8,128)(2,1)S(1)}, bf16[3072,128]{1,0:T(8,128)(2,1)}, u32[]{:S(2)}) copy-start(bf16[3072,128]{1,0:T(8,128)(2,1)} %k_hbm.1) | copy-start | bytes 2359300
  4.1 1.1 %copy-start.3 = (bf16[3072,128]{1,0:T(8,128)(2,1)S(1)}, bf16[3072,128]{1,0:T(8,128)(2,1)}, u32[]{:S(2)}) copy-start(bf16[3072,128]{1,0:T(8,128)(2,1)} %v_hbm.1) | copy-start | bytes 2359300
  5.3 0.7 %copy-start.4 = (f32[128]{0:T(128)S(1)}, f32[128]{0:T(128)}, u32[]{:S(2)}) copy-start(f32[128]{0:T(128)} %param.10) | copy-start | bytes 1540

commit v2 on v1

v2 whole, which is shorter than its diff:
```python
import jax
import jax.numpy as jnp
from jax import lax
from jax.experimental import pallas as pl
from jax.experimental.pallas import tpu as pltpu
from jax.sharding import PartitionSpec as P

MESH = pl.DeviceIdType.MESH
HD = 128
X, Y, Z, CORES = 4, 4, 8, 2
HEADS = Y * CORES
ROWS = 3072
COLS = 512
SUB = 256
SUBS = ROWS // SUB
LATE = (512, 512, 512, 512)
EARLY = ROWS - sum(LATE)
EARLY_HALF = EARLY // 2
LATE_FROM = tuple(EARLY + sum(LATE[:i]) for i in range(len(LATE)))
STATE_ROWS = HD + 16
LOCAL_AT, STATE_AT, NORMED_AT = EARLY, 2 * EARLY, 2 * EARLY + STATE_ROWS
SHIFT = NORMED_AT - EARLY
GATHERED = ROWS + SHIFT
PARTS = [
    (0, EARLY_HALF),
    (EARLY_HALF, EARLY_HALF),
    (LOCAL_AT, EARLY_HALF),
    (LOCAL_AT + EARLY_HALF, EARLY_HALF),
    (STATE_AT, STATE_ROWS),
] + [(SHIFT + start, count) for start, count in zip(LATE_FROM, LATE)]
STATE, FIRST_LATE = 4, 5
DIRECT = (STATE,)
BESIDE_FIRST = 4
AHEAD_GIVEN, LATER_GIVEN = 3, 1
AHEAD_Z = 3
STEP = EARLY // 4
QUARTER = HD // X
NT = (((1,), (1,)), ((), ()))
TN = (((0,), (0,)), ((), ()))
F32, BF16 = jnp.float32, jnp.bfloat16

FROM_LEFT, FROM_RIGHT, FAR_A, FAR_B, SIB_OWN, SIB_LEFT, SIB_RIGHT, SIB_A, SIB_B = range(9)


def split_two(x):
    high = x.astype(BF16)
    return jnp.concatenate([high, (x - high.astype(F32)).astype(BF16)], axis=1)


def dot_two(rows, halves):
    both = jnp.dot(rows, halves, preferred_element_type=F32)
    return both[:, :HD] + both[:, HD:]


def normalize(attended, gain):
    mean_square = jnp.mean(attended * attended, axis=-1, keepdims=True)
    return (attended * lax.rsqrt(mean_square + 1e-06) * gain).astype(BF16)


def kernel(
    q_hbm, k_hbm, v_hbm, prefix_ref, gain_hbm, w_hbm, out,
    q, k, v, w, gain_ref, local, gathered, total, earlier, own_masked, read_state,
    got1, sums, got2, give3, got3,
    near_sem, far_sem, load_sem, ex_send, ex_recv, ring_send, ring_recv,
):
    ctx, head = lax.axis_index("ctx"), lax.axis_index("head")
    z, x = ctx // X, ctx % X
    y, core = head // CORES, head % CORES

    x_peers = [(z * X + (x + s) % X, head) for s in range(1, X)]
    z_peers = [(((z + s) % Z) * X + x, head) for s in range(1, Z)]
    up, down = (y + 1) % Y, (y + Y - 1) % Y
    right, left = (ctx, up * CORES + core), (ctx, down * CORES + core)
    far = (ctx, ((y + 2) % Y) * CORES + core)
    sibling = (ctx, y * CORES + 1 - core)

    barrier = pltpu.get_barrier_semaphore()
    for s in range(1, Y):
        pl.semaphore_signal(
            barrier, inc=1, device_id=(ctx, ((y + s) % Y) * CORES), device_id_type=MESH
        )

    @pl.when(core == 1)
    def _():
        pl.semaphore_signal(barrier, inc=1, device_id=sibling, device_id_type=MESH)

    for peer in x_peers:
        pl.semaphore_signal(barrier, inc=1, device_id=peer, device_id_type=MESH)
    for peer, _ in z_peers:
        pl.semaphore_signal(barrier, inc=1, device_id=(peer, y * CORES + 1), device_id_type=MESH)

    loads = [
        pltpu.make_async_copy(src, dst, load_sem.at[i])
        for i, (src, dst) in enumerate([
            (q_hbm.at[pl.ds(0, EARLY)], gathered.at[head, pl.ds(0, EARLY)]),
            (q_hbm, q), (gain_hbm, gain_ref), (w_hbm, w),
        ] + [
            (src.at[pl.ds(i * ROWS // 2, ROWS // 2)], dst.at[pl.ds(i * ROWS // 2, ROWS // 2)])
            for i in range(2) for src, dst in ((k_hbm, k), (v_hbm, v))
        ])
    ]
    early_load, q_load, gain_load, w_load = loads[:4]
    ahead = z < AHEAD_Z
    for load in loads[4:]:
        load.start()

    far_head = ((y + 2) % Y) * CORES + core
    left_head, right_head = down * CORES + core, up * CORES + core

    def copy(part, slot):
        start, count = PARTS[part]
        direct = part in DIRECT
        upper = count if direct else (count // 2 + 15) // 16 * 16
        heads, first, count, peer = (
            (head, start, count, right),
            (head, start, count, left),
            (head, start, count, far) if direct else (left_head, start, upper, right),
            (right_head, start + upper, count - upper, left),
            (head, start, count, sibling),
            (left_head, start, count, sibling),
            (right_head, start, count, sibling),
            (far_head, start, upper, sibling),
            (far_head, start + upper, count - upper, sibling),
        )[slot]
        piece = gathered.at[heads, pl.ds(first, count)]
        return pltpu.make_async_remote_copy(
            src_ref=piece, dst_ref=piece,
            send_sem=ring_send.at[part, slot], recv_sem=ring_recv.at[part, slot],
            device_id=peer, device_id_type=MESH,
        )

    def slots(part):
        return [slot for slot in range(9) if part not in DIRECT or slot not in (FAR_B, SIB_B)]

    def give(part):
        if part in DIRECT:
            copy(part, FAR_A).start()
        for slot in (FROM_LEFT, FROM_RIGHT, SIB_OWN):
            copy(part, slot).start()

    def forward(part):
        copy(part, FROM_LEFT).wait_recv()
        if part not in DIRECT:
            copy(part, FAR_A).start()
        copy(part, SIB_LEFT).start()
        copy(part, FROM_RIGHT).wait_recv()
        if part not in DIRECT:
            copy(part, FAR_B).start()
        copy(part, SIB_RIGHT).start()

    def pass_far(part):
        copy(part, FAR_A).wait_recv()
        copy(part, SIB_A).start()
        if part not in DIRECT:
            copy(part, FAR_B).wait_recv()
            copy(part, SIB_B).start()

    def arrived(*parts):
        for part in parts:
            for slot in slots(part):
                if slot >= SIB_OWN:
                    copy(part, slot).wait_recv()

    def meet():
        @pl.when(core == 0)
        def _():
            pl.semaphore_signal(near_sem, inc=1, device_id=sibling, device_id_type=MESH)

        @pl.when(core == 1)
        def _():
            pl.semaphore_wait(near_sem, 1)

    prefix = prefix_ref[0]
    base = ctx * ROWS

    def inside(block):
        at = base + block * SUB + lax.broadcasted_iota(jnp.int32, (SUB, HD), 0)
        return at < prefix

    def state(block, carry):
        rows = pl.ds(block * SUB, SUB)
        vals = v[rows, :]
        masked = jnp.where(inside(block), vals, jnp.zeros_like(vals))
        earlier[block] = split_two(carry[:, :HD])
        return carry + lax.dot_general(
            k[rows, :], jnp.concatenate([vals, masked], axis=1), TN, preferred_element_type=F32
        )

    loads[4].wait()
    loads[5].wait()
    pl.when(ahead)(early_load.start)
    q_load.start()
    gain_load.start()
    w_load.start()
    summed = lax.fori_loop(0, SUBS // 2, state, jnp.zeros((HD, 2 * HD), F32))
    loads[6].wait()
    loads[7].wait()
    summed = lax.fori_loop(SUBS // 2, SUBS, state, summed)
    total[...] = summed
    own_masked[...] = split_two(summed[:, HD:])
    mine = pl.ds(pl.multiple_of(x * QUARTER, QUARTER), QUARTER)
    got1[x] = total[mine, :]

    row_at = lax.broadcasted_iota(jnp.int32, (SUB, SUB), 0)
    col_at = lax.broadcasted_iota(jnp.int32, (SUB, SUB), 1)

    def causal(block, _):
        rows = pl.ds(block * SUB, SUB)
        queries = q[rows, :]
        scores = lax.dot_general(queries, k[rows, :], NT, preferred_element_type=F32)
        weights = jnp.where(col_at <= row_at, scores, 0.0).astype(BF16)
        near = jnp.dot(weights, v[rows, :], preferred_element_type=F32)
        near = near + dot_two(queries, earlier[block])
        local[rows, :] = jnp.where(inside(block), dot_two(queries, own_masked[...]), near)
        return 0

    def give_local():
        for half in range(2):
            rows = slice(half * EARLY_HALF, (half + 1) * EARLY_HALF)
            at = LOCAL_AT + half * EARLY_HALF
            gathered[head, at:at + EARLY_HALF, :] = local[rows, :].astype(BF16)
            give(2 + half)

    @pl.when(core == 0)
    def _():
        pl.semaphore_wait(barrier, 1 + (Y - 1) * CORES + X - 1)

    @pl.when(ahead)
    def _():
        meet()
        early_load.wait()
        give(0)
        give(1)
        q_load.wait()
        lax.fori_loop(0, EARLY // SUB, causal, 0)
        give_local()


    @pl.when(core == 1)
    def _():
        pl.semaphore_wait(barrier, CORES * (Z - 1) + X - 1)

    def exchange(src, dst, slot, peer):
        return pltpu.make_async_remote_copy(
            src_ref=src, dst_ref=dst, send_sem=ex_send.at[slot], recv_sem=ex_recv.at[slot],
            device_id=peer, device_id_type=MESH,
        )

    first = []
    for s in range(1, X):
        quarter = pl.ds(pl.multiple_of(((x + s) % X) * QUARTER, QUARTER), QUARTER)
        first.append(exchange(total.at[quarter], got1.at[x], s - 1, x_peers[s - 1]))
        first[-1].start()

    @pl.when(~ahead)
    def _():
        meet()

    @pl.when(core == 1)
    def _():
        pl.semaphore_signal(far_sem, inc=1, device_id=sibling, device_id_type=MESH)

    @pl.when(~ahead)
    def _():
        q_load.wait()
        lax.fori_loop(0, BESIDE_FIRST, causal, 0)

    @pl.when(ahead)
    def _():
        forward(0)

    for moved in first:
        moved.wait_recv()
    along_x = got1[0] + got1[1] + got1[2] + got1[3]
    sums[0] = along_x[:, :HD].astype(BF16)
    sums[1] = along_x[:, HD:].astype(BF16)

    @pl.when(core == 0)
    def _():
        pl.semaphore_wait(far_sem, 1)

    second = []
    for s in range(1, Z):
        second.append(exchange(sums.at[(z + s) // Z], got2.at[s - 1], X - 2 + s, z_peers[s - 1]))
        second[-1].start()

    @pl.when(ahead)
    def _():
        lax.fori_loop(EARLY // SUB, SUBS, causal, 0)
        forward(1)

    @pl.when(~ahead)
    def _():
        lax.fori_loop(BESIDE_FIRST, SUBS, causal, 0)

    for moved in second:
        moved.wait_recv()
    along_z = got2[0].astype(F32)
    for s in range(1, Z - 1):
        along_z = along_z + got2[s].astype(F32)
    for to in range(X):
        part = along_z
        for s in range(X):
            if s < to:
                part = part + got1[s][:, :HD]
            elif s > to:
                part = part + got1[s][:, HD:]
        give3[to] = part
    got3[x] = give3[x]

    third = []
    for s in range(1, X):
        third.append(exchange(give3.at[(x + s) % X], got3.at[x], X + Z - 3 + s, x_peers[s - 1]))
        third[-1].start()

    @pl.when(ahead)
    def _():
        forward(2)
        forward(3)

    for moved in third:
        moved.wait_recv()
    read_state[...] = split_two(got3[...].reshape(HD, HD))

    gain_load.wait()
    gain = gain_ref[...]

    def give_state():
        gathered[head, STATE_AT:STATE_AT + HD, :] = read_state[:, :HD]
        gain_high = gain.astype(BF16).astype(F32)
        gain_row = lax.broadcasted_iota(jnp.int32, (16, HD), 0)
        gathered[head, STATE_AT + HD:NORMED_AT, :] = jnp.where(
            gain_row == 0, gain_high, jnp.where(gain_row == 1, gain - gain_high, 0.0)
        ).astype(BF16)
        give(STATE)

    def rows_of(part):
        start, count = PARTS[part]
        start = start - SHIFT if part >= FIRST_LATE else start
        return slice(start, start + count)

    def place_of(part):
        start, count = PARTS[part]
        return slice(start, start + count)

    def norm(part):
        rows = rows_of(part)
        attended = dot_two(q[rows, :], read_state[...]) + local[rows, :]
        gathered[head, place_of(part), :] = normalize(attended, gain)
        give(part)

    def project(part):
        normed = jnp.concatenate([gathered[h, place_of(part), :] for h in range(HEADS)], axis=1)
        out[rows_of(part), :] = jnp.dot(normed, w[...], preferred_element_type=F32).astype(BF16)

    def early(step, _):
        rows = pl.ds(pl.multiple_of(step * STEP, 16), STEP)
        local_rows = pl.ds(pl.multiple_of(LOCAL_AT + step * STEP, 16), STEP)
        normed = []
        for h in range(HEADS):
            gains = gathered[h, STATE_AT + HD:NORMED_AT, :].astype(F32)
            attended = jnp.dot(
                gathered[h, rows, :], gathered[h, STATE_AT:STATE_AT + HD, :], preferred_element_type=F32
            ) + gathered[h, local_rows, :].astype(F32)
            normed.append(normalize(attended, gains[0:1] + gains[1:2]))
        out[rows, :] = jnp.dot(
            jnp.concatenate(normed, axis=1), w[...], preferred_element_type=F32
        ).astype(BF16)
        return 0

    w_load.wait()
    late = list(range(FIRST_LATE, len(PARTS)))

    def drain(parts):
        for part in parts:
            for slot in slots(part):
                copy(part, slot).wait_send()

    def stream(parts, given, between):
        for i, part in enumerate(parts):
            if i + given < len(parts):
                norm(parts[i + given])
            forward(part)
            between(i)
            if i > 1:
                arrived(parts[i - 2])
                project(parts[i - 2])
            if i > 0:
                pass_far(parts[i - 1])
        arrived(parts[-2])
        project(parts[-2])
        pass_far(parts[-1])
        arrived(parts[-1])
        project(parts[-1])

    @pl.when(ahead)
    def _():
        give_state()
        for part in late[:AHEAD_GIVEN]:
            norm(part)
        for part in range(4):
            pass_far(part)
        forward(STATE)
        pass_far(STATE)
        arrived(0, 2, STATE)
        lax.fori_loop(0, 2, early, 0)

        def between(i):
            if i == 0:
                arrived(1, 3)
                lax.fori_loop(2, 4, early, 0)

        stream(late, AHEAD_GIVEN, between)
        drain(range(len(PARTS)))

    @pl.when(~ahead)
    def _():
        parts = [0, 1] + late
        for part in parts[:LATER_GIVEN]:
            norm(part)
        stream(parts, LATER_GIVEN, lambda i: None)
        drain(parts)

    for moved in first + second + third:
        moved.wait_send()


def body(queries, keys, values, prefix, norm_gain, out_weight):
    def hbm(array):
        return pltpu.with_memory_space_constraint(array, pltpu.HBM)

    anywhere = pl.BlockSpec(memory_space=pl.ANY)
    exchanges = 2 * (X - 1) + Z - 1
    return pl.pallas_call(
        kernel,
        out_shape=pltpu.VMEM((ROWS, COLS), BF16),
        in_specs=[
            anywhere, anywhere, anywhere,
            pl.BlockSpec(memory_space=pltpu.SMEM),
            anywhere, anywhere,
        ],
        out_specs=pl.BlockSpec(memory_space=pltpu.VMEM),
        scratch_shapes=[
            pltpu.VMEM((ROWS, HD), BF16),
            pltpu.VMEM((ROWS, HD), BF16),
            pltpu.VMEM((ROWS, HD), BF16),
            pltpu.VMEM((HEADS * HD, COLS), BF16),
            pltpu.VMEM((1, HD), F32),
            pltpu.VMEM((ROWS, HD), F32),
            pltpu.VMEM((HEADS, GATHERED, HD), BF16),
            pltpu.VMEM((HD, 2 * HD), F32),
            pltpu.VMEM((SUBS, HD, 2 * HD), BF16),
            pltpu.VMEM((HD, 2 * HD), BF16),
            pltpu.VMEM((HD, 2 * HD), BF16),
            pltpu.VMEM((X, QUARTER, 2 * HD), F32),
            pltpu.VMEM((2, QUARTER, HD), BF16),
            pltpu.VMEM((Z - 1, QUARTER, HD), BF16),
            pltpu.VMEM((X, QUARTER, HD), F32),
            pltpu.VMEM((X, QUARTER, HD), F32),
            pltpu.SemaphoreType.REGULAR,
            pltpu.SemaphoreType.REGULAR,
            pltpu.SemaphoreType.DMA((8,)),
            pltpu.SemaphoreType.DMA((exchanges,)),
            pltpu.SemaphoreType.DMA((exchanges,)),
            pltpu.SemaphoreType.DMA((len(PARTS), 9)),
            pltpu.SemaphoreType.DMA((len(PARTS), 9)),
        ],
        compiler_params=pltpu.CompilerParams(
            collective_id=0, has_side_effects=True, vmem_limit_bytes=40 * 2**20
        ),
        cost_estimate=pl.CostEstimate(
            flops=2 * ROWS * (8 * HD * COLS + 1024 * HD), bytes_accessed=8 * 2**20, transcendentals=ROWS
        ),
    )(hbm(queries), hbm(keys), hbm(values), prefix, hbm(norm_gain.reshape(1, HD)), hbm(out_weight))


def solution(mesh):
    return jax.shard_map(
        body,
        mesh=mesh,
        in_specs=(
            P("ctx", "head"),
            P("ctx", "head"),
            P("ctx", "head"),
            P(),
            P("head"),
            P(None, "head"),
        ),
        out_specs=P("ctx", "head"),
        check_vma=False,
    )
```

time: 62.5 us -> 53.5 us (0.86)
  local copies, waits for them, and re-layouts: 6.94 us -> 1.67 us
  Pallas kernels: 54.6 us -> 50.6 us
    unnamed x11 -> x1, local copies, waits for them, and re-layouts: 6.94 us -> 1.67 us
    pallas_call x1, Pallas kernels: 54.6 us -> 50.6 us  [body(): pl.pallas_call(kernel, out_shape=pltpu.VMEM((ROWS, COLS), BF16), in_specs...]
where the time goes in v2:
time: 53.5 us; the launch traced here: 52.9 us
  Pallas kernels  50.6 us (95%)
  local copies, waits for them, and re-layouts  1.67 us (3%)
  between operations  0.66 us (1%)
    pallas_call x1, Pallas kernels, body(): pl.pallas_call(kernel, out_shape=pltpu.VMEM((ROWS, COLS), BF16), in_specs...  50.6 us
    unnamed x1, local copies, waits for them, and re-layouts  1.67 us

profile of v2, /device:TPU:1, one launch (start us, length us, event | category | flops | bytes accessed | tf_op | source)
XLA Modules:
  0.0 52.9 jit_solution(4382627427195152778)
XLA Ops:
  0.7 50.6 %shard_map.64 = bf16[3072,512]{1,0:T(8,128)(2,1)S(1)} custom-call(bf16[3072,128]{1,0:T(8,128)(2,1)} %q_hbm.1, bf16[3072,128]{1,0:T(8,128)(2,1)} %k_hbm.1, bf16[3072,128]{1,0:T(8,128)(2,1)} %v_hbm.1, s32[1]{0:T(128)S(6)} %copy.9.prefix_ref, f32[1,128]{1,0:T(1,128)} %bitcast.1, bf16[1024,512]{1,0:T(8,128)(2,1)} %w_hbm.1), custom_call_target="tpu_custom_call" | custom-call | flops 4026531840 | bytes 8388608 | tf_op jit(solution)/shard_map/pallas_call | solution.py:434
  51.2 1.7 %copy.8 = bf16[3072,512]{1,0:T(8,128)(2,1)} copy(bf16[3072,512]{1,0:T(8,128)(2,1)S(1)} %shard_map.64) | data formatting | bytes 6291456

commit v3 on v2

--- a/solution.py
+++ b/solution.py
@@ -13,27 +13,20 @@
 COLS = 512
 SUB = 256
 SUBS = ROWS // SUB
-LATE = (512, 512, 512, 512)
-EARLY = ROWS - sum(LATE)
-EARLY_HALF = EARLY // 2
-LATE_FROM = tuple(EARLY + sum(LATE[:i]) for i in range(len(LATE)))
+UNIT = 512
+UNITS = ROWS // UNIT
+STEPS = UNIT // SUB
+AHEAD_Z, EARLY_AHEAD, EARLY_ELSE = 3, 2, 1
+GIVEN_AHEAD, GIVEN_ELSE = 2, 2
+BESIDE_FIRST = 4
 STATE_ROWS = HD + 16
-LOCAL_AT, STATE_AT, NORMED_AT = EARLY, 2 * EARLY, 2 * EARLY + STATE_ROWS
-SHIFT = NORMED_AT - EARLY
-GATHERED = ROWS + SHIFT
-PARTS = [
-    (0, EARLY_HALF),
-    (EARLY_HALF, EARLY_HALF),
-    (LOCAL_AT, EARLY_HALF),
-    (LOCAL_AT + EARLY_HALF, EARLY_HALF),
-    (STATE_AT, STATE_ROWS),
-] + [(SHIFT + start, count) for start, count in zip(LATE_FROM, LATE)]
-STATE, FIRST_LATE = 4, 5
+STATE_AT = ROWS + EARLY_AHEAD * UNIT
+GAIN_AT = STATE_AT + HD
+GATHERED = STATE_AT + STATE_ROWS
+LOCALS = UNITS
+STATE = UNITS + EARLY_AHEAD
+PARTS = [(i * UNIT, UNIT) for i in range(UNITS + EARLY_AHEAD)] + [(STATE_AT, STATE_ROWS)]
 DIRECT = (STATE,)
-BESIDE_FIRST = 4
-AHEAD_GIVEN, LATER_GIVEN = 3, 1
-AHEAD_Z = 3
-STEP = EARLY // 4
 QUARTER = HD // X
 NT = (((1,), (1,)), ((), ()))
 TN = (((0,), (0,)), ((), ()))
@@ -92,7 +85,7 @@
     loads = [
         pltpu.make_async_copy(src, dst, load_sem.at[i])
         for i, (src, dst) in enumerate([
-            (q_hbm.at[pl.ds(0, EARLY)], gathered.at[head, pl.ds(0, EARLY)]),
+            (q_hbm.at[pl.ds(0, EARLY_AHEAD * UNIT)], gathered.at[head, pl.ds(0, EARLY_AHEAD * UNIT)]),
             (q_hbm, q), (gain_hbm, gain_ref), (w_hbm, w),
         ] + [
             (src.at[pl.ds(i * ROWS // 2, ROWS // 2)], dst.at[pl.ds(i * ROWS // 2, ROWS // 2)])
@@ -188,7 +181,7 @@
 
     loads[4].wait()
     loads[5].wait()
-    pl.when(ahead)(early_load.start)
+    early_load.start()
     q_load.start()
     gain_load.start()
     w_load.start()
@@ -214,12 +207,11 @@
         local[rows, :] = jnp.where(inside(block), dot_two(queries, own_masked[...]), near)
         return 0
 
-    def give_local():
-        for half in range(2):
-            rows = slice(half * EARLY_HALF, (half + 1) * EARLY_HALF)
-            at = LOCAL_AT + half * EARLY_HALF
-            gathered[head, at:at + EARLY_HALF, :] = local[rows, :].astype(BF16)
-            give(2 + half)
+    def give_local(unit):
+        lax.fori_loop(unit * STEPS, (unit + 1) * STEPS, causal, 0)
+        rows = slice(unit * UNIT, (unit + 1) * UNIT)
+        gathered[head, ROWS + rows.start:ROWS + rows.stop, :] = local[rows, :].astype(BF16)
+        give(LOCALS + unit)
 
     @pl.when(core == 0)
     def _():
@@ -229,11 +221,9 @@
     def _():
         meet()
         early_load.wait()
-        give(0)
-        give(1)
+        for unit in range(EARLY_AHEAD):
+            give(unit)
         q_load.wait()
-        lax.fori_loop(0, EARLY // SUB, causal, 0)
-        give_local()
 
 
     @pl.when(core == 1)
@@ -260,14 +250,20 @@
     def _():
         pl.semaphore_signal(far_sem, inc=1, device_id=sibling, device_id_type=MESH)
 
+    @pl.when(ahead)
+    def _():
+        for unit in range(EARLY_AHEAD):
+            give_local(unit)
+
     @pl.when(~ahead)
     def _():
+        early_load.wait()
+        for unit in range(EARLY_ELSE):
+            give(unit)
         q_load.wait()
-        lax.fori_loop(0, BESIDE_FIRST, causal, 0)
-
-    @pl.when(ahead)
-    def _():
-        forward(0)
+        for unit in range(EARLY_ELSE):
+            give_local(unit)
+        lax.fori_loop(EARLY_ELSE * STEPS, BESIDE_FIRST, causal, 0)
 
     for moved in first:
         moved.wait_recv()
@@ -286,12 +282,14 @@
 
     @pl.when(ahead)
     def _():
-        lax.fori_loop(EARLY // SUB, SUBS, causal, 0)
+        forward(0)
+        lax.fori_loop(EARLY_AHEAD * STEPS, SUBS, causal, 0)
         forward(1)
 
     @pl.when(~ahead)
     def _():
         lax.fori_loop(BESIDE_FIRST, SUBS, causal, 0)
+        forward(0)
 
     for moved in second:
         moved.wait_recv()
@@ -315,8 +313,12 @@
 
     @pl.when(ahead)
     def _():
-        forward(2)
-        forward(3)
+        forward(LOCALS)
+        forward(LOCALS + 1)
+
+    @pl.when(~ahead)
+    def _():
+        forward(LOCALS)
 
     for moved in third:
         moved.wait_recv()
@@ -326,41 +328,37 @@
     gain = gain_ref[...]
 
     def give_state():
-        gathered[head, STATE_AT:STATE_AT + HD, :] = read_state[:, :HD]
+        gathered[head, STATE_AT:GAIN_AT, :] = read_state[:, :HD]
         gain_high = gain.astype(BF16).astype(F32)
         gain_row = lax.broadcasted_iota(jnp.int32, (16, HD), 0)
-        gathered[head, STATE_AT + HD:NORMED_AT, :] = jnp.where(
+        gathered[head, GAIN_AT:GATHERED, :] = jnp.where(
             gain_row == 0, gain_high, jnp.where(gain_row == 1, gain - gain_high, 0.0)
         ).astype(BF16)
         give(STATE)
 
-    def rows_of(part):
-        start, count = PARTS[part]
-        start = start - SHIFT if part >= FIRST_LATE else start
-        return slice(start, start + count)
-
-    def place_of(part):
-        start, count = PARTS[part]
-        return slice(start, start + count)
-
-    def norm(part):
-        rows = rows_of(part)
+    def norm(unit):
+        rows = slice(unit * UNIT, (unit + 1) * UNIT)
         attended = dot_two(q[rows, :], read_state[...]) + local[rows, :]
-        gathered[head, place_of(part), :] = normalize(attended, gain)
-        give(part)
-
-    def project(part):
-        normed = jnp.concatenate([gathered[h, place_of(part), :] for h in range(HEADS)], axis=1)
-        out[rows_of(part), :] = jnp.dot(normed, w[...], preferred_element_type=F32).astype(BF16)
+        gathered[head, rows, :] = normalize(attended, gain)
+        give(unit)
+
+    def project(unit):
+        def one(step, _):
+            rows = pl.ds(pl.multiple_of(step * SUB, SUB), SUB)
+            normed = jnp.concatenate([gathered[h, rows, :] for h in range(HEADS)], axis=1)
+            out[rows, :] = jnp.dot(normed, w[...], preferred_element_type=F32).astype(BF16)
+            return 0
+
+        lax.fori_loop(unit * STEPS, (unit + 1) * STEPS, one, 0)
 
     def early(step, _):
-        rows = pl.ds(pl.multiple_of(step * STEP, 16), STEP)
-        local_rows = pl.ds(pl.multiple_of(LOCAL_AT + step * STEP, 16), STEP)
+        rows = pl.ds(pl.multiple_of(step * SUB, SUB), SUB)
+        local_rows = pl.ds(pl.multiple_of(ROWS + step * SUB, SUB), SUB)
         normed = []
         for h in range(HEADS):
-            gains = gathered[h, STATE_AT + HD:NORMED_AT, :].astype(F32)
+            gains = gathered[h, GAIN_AT:GATHERED, :].astype(F32)
             attended = jnp.dot(
-                gathered[h, rows, :], gathered[h, STATE_AT:STATE_AT + HD, :], preferred_element_type=F32
+                gathered[h, rows, :], gathered[h, STATE_AT:GAIN_AT, :], preferred_element_type=F32
             ) + gathered[h, local_rows, :].astype(F32)
             normed.append(normalize(attended, gains[0:1] + gains[1:2]))
         out[rows, :] = jnp.dot(
@@ -369,60 +367,60 @@
         return 0
 
     w_load.wait()
-    late = list(range(FIRST_LATE, len(PARTS)))
-
-    def drain(parts):
-        for part in parts:
-            for slot in slots(part):
+
+    def drain(part, which=range(9)):
+        for slot in slots(part):
+            if slot in which:
                 copy(part, slot).wait_send()
 
-    def stream(parts, given, between):
-        for i, part in enumerate(parts):
-            if i + given < len(parts):
-                norm(parts[i + given])
-            forward(part)
-            between(i)
-            if i > 1:
-                arrived(parts[i - 2])
-                project(parts[i - 2])
-            if i > 0:
-                pass_far(parts[i - 1])
-        arrived(parts[-2])
-        project(parts[-2])
-        pass_far(parts[-1])
-        arrived(parts[-1])
-        project(parts[-1])
-
-    @pl.when(ahead)
-    def _():
+    def finish(early_units, given):
+        units = list(range(early_units, UNITS))
+        before = [part for unit in range(early_units) for part in (unit, LOCALS + unit)]
         give_state()
-        for part in late[:AHEAD_GIVEN]:
-            norm(part)
-        for part in range(4):
+        for unit in units[:given]:
+            norm(unit)
+        for part in before:
             pass_far(part)
         forward(STATE)
         pass_far(STATE)
-        arrived(0, 2, STATE)
-        lax.fori_loop(0, 2, early, 0)
-
-        def between(i):
-            if i == 0:
-                arrived(1, 3)
-                lax.fori_loop(2, 4, early, 0)
-
-        stream(late, AHEAD_GIVEN, between)
-        drain(range(len(PARTS)))
+        arrived(STATE)
+        sent = before + [STATE]
+        for i, unit in enumerate(units):
+            if i < early_units:
+                arrived(i, LOCALS + i)
+                lax.fori_loop(i * STEPS, (i + 1) * STEPS, early, 0)
+            if i + given < len(units):
+                norm(units[i + given])
+            forward(unit)
+            if i > 1:
+                arrived(units[i - 2])
+                project(units[i - 2])
+            if i > 0:
+                pass_far(units[i - 1])
+                for part in sent[:2]:
+                    drain(part)
+                sent = sent[2:]
+            else:
+                for moved in first + second + third:
+                    moved.wait_send()
+        for part in sent + units[:-2]:
+            drain(part)
+        arrived(units[-2])
+        project(units[-2])
+        pass_far(units[-1])
+        drain(units[-2])
+        drain(units[-1], range(SIB_A))
+        arrived(units[-1])
+        project(units[-1])
+        drain(units[-1], (SIB_A, SIB_B))
+
+    @pl.when(ahead)
+    def _():
+        finish(EARLY_AHEAD, GIVEN_AHEAD)
 
     @pl.when(~ahead)
     def _():
-        parts = [0, 1] + late
-        for part in parts[:LATER_GIVEN]:
-            norm(part)
-        stream(parts, LATER_GIVEN, lambda i: None)
-        drain(parts)
-
-    for moved in first + second + third:
-        moved.wait_send()
+        finish(EARLY_ELSE, GIVEN_ELSE)
 
 
 def body(queries, keys, values, prefix, norm_gain, out_weight):

time: 53.5 us -> 52.6 us (0.983)
  no operation moved by 1% of the time
where the time goes in v3:
time: 52.6 us; the launch traced here: 52.5 us
  Pallas kernels  50.2 us (95%)
  local copies, waits for them, and re-layouts  1.67 us (3%)
  between operations  0.66 us (1%)
    pallas_call x1, Pallas kernels, body(): pl.pallas_call(kernel, out_shape=pltpu.VMEM((ROWS, COLS), BF16), in_specs...  50.2 us
    unnamed x1, local copies, waits for them, and re-layouts  1.67 us

profile of v3, /device:TPU:1, one launch (start us, length us, event | category | flops | bytes accessed | tf_op | source)
XLA Modules:
  0.0 52.5 jit_solution(3980222890066997596)
XLA Ops:
  0.7 50.2 %shard_map.64 = bf16[3072,512]{1,0:T(8,128)(2,1)S(1)} custom-call(bf16[3072,128]{1,0:T(8,128)(2,1)} %q_hbm.1, bf16[3072,128]{1,0:T(8,128)(2,1)} %k_hbm.1, bf16[3072,128]{1,0:T(8,128)(2,1)} %v_hbm.1, s32[1]{0:T(128)S(6)} %copy.9.prefix_ref, f32[1,128]{1,0:T(1,128)} %bitcast.1, bf16[1024,512]{1,0:T(8,128)(2,1)} %w_hbm.1), custom_call_target="tpu_custom_call" | custom-call | flops 4026531840 | bytes 8388608 | tf_op jit(solution)/shard_map/pallas_call | solution.py:432
  50.8 1.7 %copy.8 = bf16[3072,512]{1,0:T(8,128)(2,1)} copy(bf16[3072,512]{1,0:T(8,128)(2,1)S(1)} %shard_map.64) | data formatting | bytes 6291456

commit v4 on v3

--- a/solution.py
+++ b/solution.py
@@ -393,18 +393,22 @@
                 norm(units[i + given])
             forward(unit)
             if i > 1:
-                arrived(units[i - 2])
-                project(units[i - 2])
+                pass_far(units[i - 2])
+            if i > 2:
+                arrived(units[i - 3])
+                project(units[i - 3])
             if i > 0:
-                pass_far(units[i - 1])
                 for part in sent[:2]:
                     drain(part)
                 sent = sent[2:]
             else:
                 for moved in first + second + third:
                     moved.wait_send()
+        pass_far(units[-2])
         for part in sent + units[:-2]:
             drain(part)
+        arrived(units[-3])
+        project(units[-3])
         arrived(units[-2])
         project(units[-2])
         pass_far(units[-1])

time: 52.6 us -> 51.8 us (0.985)
  Pallas kernels: 50.2 us -> 49.3 us
    pallas_call x1, Pallas kernels: 50.2 us -> 49.3 us  [body(): pl.pallas_call(kernel, out_shape=pltpu.VMEM((ROWS, COLS), BF16), in_specs...]
where the time goes in v4:
time: 51.8 us; the launch traced here: 51.7 us
  Pallas kernels  49.3 us (95%)
  local copies, waits for them, and re-layouts  1.67 us (3%)
  between operations  0.66 us (1%)
    pallas_call x1, Pallas kernels, body(): pl.pallas_call(kernel, out_shape=pltpu.VMEM((ROWS, COLS), BF16), in_specs...  49.3 us
    unnamed x1, local copies, waits for them, and re-layouts  1.67 us

profile of v4, /device:TPU:1, one launch (start us, length us, event | category | flops | bytes accessed | tf_op | source)
XLA Modules:
  0.0 51.7 jit_solution(7949906930189156176)
XLA Ops:
  0.7 49.3 %shard_map.64 = bf16[3072,512]{1,0:T(8,128)(2,1)S(1)} custom-call(bf16[3072,128]{1,0:T(8,128)(2,1)} %q_hbm.1, bf16[3072,128]{1,0:T(8,128)(2,1)} %k_hbm.1, bf16[3072,128]{1,0:T(8,128)(2,1)} %v_hbm.1, s32[1]{0:T(128)S(6)} %copy.9.prefix_ref, f32[1,128]{1,0:T(1,128)} %bitcast.1, bf16[1024,512]{1,0:T(8,128)(2,1)} %w_hbm.1), custom_call_target="tpu_custom_call" | custom-call | flops 4026531840 | bytes 8388608 | tf_op jit(solution)/shard_map/pallas_call | solution.py:436
  50.0 1.7 %copy.8 = bf16[3072,512]{1,0:T(8,128)(2,1)} copy(bf16[3072,512]{1,0:T(8,128)(2,1)S(1)} %shard_map.64) | data formatting | bytes 6291456

commit v5 on v4

--- a/solution.py
+++ b/solution.py
@@ -383,15 +383,14 @@
             pass_far(part)
         forward(STATE)
         pass_far(STATE)
-        arrived(STATE)
         sent = before + [STATE]
         for i, unit in enumerate(units):
-            if i < early_units:
-                arrived(i, LOCALS + i)
-                lax.fori_loop(i * STEPS, (i + 1) * STEPS, early, 0)
             if i + given < len(units):
                 norm(units[i + given])
             forward(unit)
+            if i < early_units:
+                arrived(i, LOCALS + i, *([STATE] if i == 0 else []))
+                lax.fori_loop(i * STEPS, (i + 1) * STEPS, early, 0)
             if i > 1:
                 pass_far(units[i - 2])
             if i > 2:

time: 51.8 us -> 52.1 us (level)
  no operation moved by 1% of the time
where the time goes in v5:
time: 52.1 us; the launch traced here: 52 us
  Pallas kernels  49.7 us (95%)
  local copies, waits for them, and re-layouts  1.67 us (3%)
  between operations  0.66 us (1%)
    pallas_call x1, Pallas kernels, body(): pl.pallas_call(kernel, out_shape=pltpu.VMEM((ROWS, COLS), BF16), in_specs...  49.7 us
    unnamed x1, local copies, waits for them, and re-layouts  1.67 us

profile of v5, /device:TPU:1, one launch (start us, length us, event | category | flops | bytes accessed | tf_op | source)
XLA Modules:
  0.0 52.0 jit_solution(5530645751021674818)
XLA Ops:
  0.7 49.7 %shard_map.64 = bf16[3072,512]{1,0:T(8,128)(2,1)S(1)} custom-call(bf16[3072,128]{1,0:T(8,128)(2,1)} %q_hbm.1, bf16[3072,128]{1,0:T(8,128)(2,1)} %k_hbm.1, bf16[3072,128]{1,0:T(8,128)(2,1)} %v_hbm.1, s32[1]{0:T(128)S(6)} %copy.9.prefix_ref, f32[1,128]{1,0:T(1,128)} %bitcast.1, bf16[1024,512]{1,0:T(8,128)(2,1)} %w_hbm.1), custom_call_target="tpu_custom_call" | custom-call | flops 4026531840 | bytes 8388608 | tf_op jit(solution)/shard_map/pallas_call | solution.py:435
  50.4 1.7 %copy.8 = bf16[3072,512]{1,0:T(8,128)(2,1)} copy(bf16[3072,512]{1,0:T(8,128)(2,1)S(1)} %shard_map.64) | data formatting | bytes 6291456
